TPU v7x, 256 devices: a whole 4x4x8 slice. The times are simulated.
256 devices in a mesh: dom: 64 (over x, z, core), sub: 4 (over y).
Axes of the slice: x: 4, y: 4, z: 8, core: 2. Of those that a mesh axis runs over, the one named last changes fastest.
Arguments:
- positions: float32 [3, 2097152], P(None, ('dom', 'sub')), may hold values from 0 to 1
- masses: float32 [2097152], P(('dom', 'sub')), may hold values from 0.00029296876 to 0.0029296875
- cell_mass: float32 [32768], P(('dom', 'sub')), may hold values from 0.00234375 to 0.0234375
- cell_center: float32 [3, 32768], P(None, ('dom', 'sub')), may hold values from 0 to 1
- cell_quad: float32 [6, 32768], P(None, ('dom', 'sub')), may hold values from -0.0046875 to 0.0046875
- cell_list: int32 [32768, 128], P(('dom', 'sub')), may hold values from 0 to 32767
- leaf_list: int32 [32768, 16], P(('dom', 'sub')), may hold values from 0 to 575, as said below
- send_list: int32 [64, 4, 8, 8], P('dom', 'sub'), may hold values from 0 to 127
- send_count: int32 [64, 4, 8], P('dom', 'sub'), may hold values from 1 to 8, as said below
Outputs:
- accel: float32 [3, 2097152], P(None, ('dom', 'sub'))
Inputs may be any that keep to these rules, and one draw needn't show every extreme that they name: `send_count`: counts fall off with the distance along the curve: an offset of one domain always carries 8 blocks, an offset of d domains at most max(1, 8 // d). `leaf_list`: each id names a block of the group's own domain or a slot of the far part that carries a block.
All inputs are finite; a program needn't handle non-finite values.
Results may differ from a plain program's by a relative error of at most 0.0003.
Values sent between devices are 32-bit elements; how exact they have to be, the bound alone decides.
A program may use at most 128 MiB of HBM per device.

v0:
```python
import jax
import jax.numpy as jnp
from jax import lax
from jax.sharding import PartitionSpec as P

LEAF = 64
LEAF_DEV = 128
NCELL = 128
NLEAF = 16
RANGE = 4
CAP = 8
softening_sq = 0.0025


def passed_along(value, axis, steps):
    count = lax.axis_size(axis)
    leading, last = (max(0, -steps), min(count, count - steps))
    return lax.ppermute(value, axis, [(source, source + steps) for source in range(leading, last)])


def direct_pull(targets, sources, weights):
    offset = sources[:, :, None, :] - targets[:, :, :, None]
    dist_sq = jnp.sum(offset * offset, axis=0) + softening_sq
    factor = weights[:, None, :] / (dist_sq * jnp.sqrt(dist_sq))
    return jnp.sum(offset * factor[None], axis=-1)


def multipole_pull(targets, moments):
    offset = targets[:, :, :, None] - moments[1:4, :, None, :]
    dist_sq = jnp.sum(offset * offset, axis=0) + softening_sq
    inv_one = 1.0 / jnp.sqrt(dist_sq)
    inv_two = inv_one * inv_one
    inv_three = inv_one * inv_two
    inv_five = inv_three * inv_two
    inv_seven = inv_five * inv_two
    quad_part = moments[4:10, :, None, :]
    q_times_x = quad_part[0] * offset[0] + quad_part[3] * offset[1] + quad_part[4] * offset[2]
    q_times_y = quad_part[3] * offset[0] + quad_part[1] * offset[1] + quad_part[5] * offset[2]
    q_times_z = quad_part[4] * offset[0] + quad_part[5] * offset[1] + quad_part[2] * offset[2]
    q_times = jnp.stack([q_times_x, q_times_y, q_times_z])
    quad_form = jnp.sum(offset * q_times, axis=0)
    mass_part = moments[0, :, None, :]
    accel_terms = (
        -mass_part * inv_three * offset + inv_five * q_times - 2.5 * inv_seven * quad_form * offset
    )
    return jnp.sum(accel_terms, axis=-1)


def group_pull(targets, essential, leaf_ids, cell_table, cell_ids):
    groups_here = leaf_ids.shape[0]
    particle_ids = (
        leaf_ids[:, :, None] * LEAF + jnp.arange(LEAF, dtype=jnp.int32)[None, None, :]
    ).reshape(groups_here, -1)
    picked = essential[:, particle_ids]
    moments = cell_table[:, cell_ids]
    return direct_pull(targets, picked[0:3], picked[3]) + multipole_pull(targets, moments)


def on_device(
    positions,
    masses,
    cell_mass,
    cell_center,
    cell_quad,
    cell_list,
    leaf_list,
    send_list,
    send_count,
):
    offset_values = list(range(-RANGE, 0)) + list(range(1, RANGE + 1))
    cell_table = jnp.concatenate([cell_mass[None], cell_center, cell_quad], axis=0)
    all_cells = lax.all_gather(cell_table, ("dom", "sub"), axis=1, tiled=True)
    packed = jnp.concatenate([positions, masses[None]], axis=0)
    nearby = lax.all_gather(packed, "sub", axis=1, tiled=True)
    chosen = send_list.reshape(2 * RANGE, CAP)
    counts = send_count.reshape(2 * RANGE)
    live = (jnp.arange(CAP, dtype=jnp.int32)[None, :] < counts[:, None]).astype(jnp.float32)
    weight = jnp.repeat(live.reshape(-1), LEAF).reshape(2 * RANGE, CAP * LEAF)
    flat_ids = (
        chosen[:, :, None] * LEAF + jnp.arange(LEAF, dtype=jnp.int32)[None, None, :]
    ).reshape(2 * RANGE, CAP * LEAF)
    outgoing = packed[:, flat_ids] * weight[None]
    pieces = []
    for slot in range(2 * RANGE):
        pieces.append(passed_along(outgoing[:, slot], "dom", offset_values[slot]))
    remote = jnp.stack(pieces, axis=1)
    essential = jnp.concatenate([nearby, remote.reshape(4, 2 * RANGE * CAP * LEAF)], axis=1)
    block_size = 8
    block_count = LEAF_DEV // block_size
    target_blocks = positions.reshape(3, block_count, block_size, LEAF).transpose(1, 0, 2, 3)
    leaf_blocks = leaf_list.reshape(block_count, block_size, NLEAF)
    cell_blocks = cell_list.reshape(block_count, block_size, NCELL)

    def one_block(inputs):
        block_targets, block_leaves, block_cells = inputs
        return group_pull(block_targets, essential, block_leaves, all_cells, block_cells)

    pulled = lax.map(one_block, (target_blocks, leaf_blocks, cell_blocks))
    return pulled.transpose(1, 0, 2, 3).reshape(3, LEAF_DEV * LEAF)


def solution(mesh):
    return jax.shard_map(
        on_device,
        mesh=mesh,
        in_specs=(
            P(None, ("dom", "sub")),
            P(("dom", "sub")),
            P(("dom", "sub")),
            P(None, ("dom", "sub")),
            P(None, ("dom", "sub")),
            P(("dom", "sub"), None),
            P(("dom", "sub"), None),
            P("dom", "sub", None, None),
            P("dom", "sub", None),
        ),
        out_specs=P(None, ("dom", "sub")),
        check_vma=False,
    )
```

profile of v0, /device:TPU:1, one launch (start us, length us, event | category | flops | bytes accessed | tf_op | source)
XLA Modules:
  0.0 975.4 jit_solution(4220310291080115131)
XLA Ops:
  10.5 12.9 %gather_fusion.2 = f32[4096,4]{1,0:T(8,128)S(1)} fusion(f32[4,8192]{0,1:T(8,128)} %copy.47, s32[4096]{0:T(1024)S(1)} %broadcast_clamp_fusion), kind=kCustom, calls=%fused_computation.2 | custom fusion | bytes 147456 | tf_op jit(solution)/shard_map/gather | solution.py:82
  52.1 10.8 %all_gather.6 = f32[4,32768]{1,0:T(4,128)S(1)} all-gather(f32[4,8192]{1,0:T(4,128)S(1)} %pad_maximum_fusion.2), channel_id=1, replica_groups=mesh['dom'=64,'sub'=4] {'sub'}, dimensions={1}, use_global_device_ids=true | all-gather | bytes 655360 | tf_op jit(solution)/shard_map/all_gather | solution.py:74
  63.7 9.8 %copy.56 = f32[4,36864]{0,1:T(8,128)} copy(f32[4,36864]{1,0:T(4,128)S(1)} %pad_maximum_fusion.1) | data formatting | bytes 1179648 | tf_op jit(solution)/shard_map/while | solution.py:98
  73.5 75.3 %all-gather.2.cloned.1.call-done = f32[10,32768]{1,0:T(8,128)} async-done(((f32[10,128]{1,0:T(8,128)}), f32[10,32768]{1,0:T(8,128)}) %all-gather.2.cloned.1.call-update) | async-done | bytes 1310736 | tf_op jit(solution)/shard_map/all_gather | solution.py:72
  148.8 9.7 copy.58
  158.5 809.3 %while.10 = (s32[]{:T(128)}, f32[16,3,8,64]{3,2,1,0:T(8,128)S(1)}, s32[16,8,16]{2,1,0:T(8,128)S(1)}, f32[4,36864]{0,1:T(8,128)}, f32[16,3,8,64]{3,2,0,1:T(8,128)...) while((s32[]{:T(128)}, f32[16,3,8,64]{3,2,1,0:T(8,128)S(1)}, s32[16,8,16]{2,1,0:T(8,128)S(1)}, ...), condition=%wide.region_6.7_spmd, body=%wide.region_0.6_spmd.sunk | while | flops 15249026 | bytes 16653933 | solution.py:98
  158.8 34.1 %gather_fusion = f32[8192,4]{1,0:T(8,128)} fusion(f32[4,36864]{0,1:T(8,128)} %get-tuple-element.193, s32[8192]{0:T(1024)S(1)} %bitcast_clamp_fusion.2), kind=kCustom, calls=%fused_computation.clone.1 | custom fusion | bytes 294912 | tf_op jit(solution)/shard_map/while/body/eval_jaxpr/gather | solution.py:54
  209.4 34.1 %gather_fusion = f32[8192,4]{1,0:T(8,128)} fusion(f32[4,36864]{0,1:T(8,128)} %get-tuple-element.193, s32[8192]{0:T(1024)S(1)} %bitcast_clamp_fusion.2), kind=kCustom, calls=%fused_computation.clone.1 | custom fusion | bytes 294912 | tf_op jit(solution)/shard_map/while/body/eval_jaxpr/gather | solution.py:54
  259.9 34.1 %gather_fusion = f32[8192,4]{1,0:T(8,128)} fusion(f32[4,36864]{0,1:T(8,128)} %get-tuple-element.193, s32[8192]{0:T(1024)S(1)} %bitcast_clamp_fusion.2), kind=kCustom, calls=%fused_computation.clone.1 | custom fusion | bytes 294912 | tf_op jit(solution)/shard_map/while/body/eval_jaxpr/gather | solution.py:54
  310.5 34.1 %gather_fusion = f32[8192,4]{1,0:T(8,128)} fusion(f32[4,36864]{0,1:T(8,128)} %get-tuple-element.193, s32[8192]{0:T(1024)S(1)} %bitcast_clamp_fusion.2), kind=kCustom, calls=%fused_computation.clone.1 | custom fusion | bytes 294912 | tf_op jit(solution)/shard_map/while/body/eval_jaxpr/gather | solution.py:54
  361.1 34.1 %gather_fusion = f32[8192,4]{1,0:T(8,128)} fusion(f32[4,36864]{0,1:T(8,128)} %get-tuple-element.193, s32[8192]{0:T(1024)S(1)} %bitcast_clamp_fusion.2), kind=kCustom, calls=%fused_computation.clone.1 | custom fusion | bytes 294912 | tf_op jit(solution)/shard_map/while/body/eval_jaxpr/gather | solution.py:54
  411.7 34.1 %gather_fusion = f32[8192,4]{1,0:T(8,128)} fusion(f32[4,36864]{0,1:T(8,128)} %get-tuple-element.193, s32[8192]{0:T(1024)S(1)} %bitcast_clamp_fusion.2), kind=kCustom, calls=%fused_computation.clone.1 | custom fusion | bytes 294912 | tf_op jit(solution)/shard_map/while/body/eval_jaxpr/gather | solution.py:54
  451.7 8.6 gather_fusion.1
  462.3 34.1 %gather_fusion = f32[8192,4]{1,0:T(8,128)} fusion(f32[4,36864]{0,1:T(8,128)} %get-tuple-element.193, s32[8192]{0:T(1024)S(1)} %bitcast_clamp_fusion.2), kind=kCustom, calls=%fused_computation.clone.1 | custom fusion | bytes 294912 | tf_op jit(solution)/shard_map/while/body/eval_jaxpr/gather | solution.py:54
  512.8 34.1 %gather_fusion = f32[8192,4]{1,0:T(8,128)} fusion(f32[4,36864]{0,1:T(8,128)} %get-tuple-element.193, s32[8192]{0:T(1024)S(1)} %bitcast_clamp_fusion.2), kind=kCustom, calls=%fused_computation.clone.1 | custom fusion | bytes 294912 | tf_op jit(solution)/shard_map/while/body/eval_jaxpr/gather | solution.py:54
  563.4 34.1 %gather_fusion = f32[8192,4]{1,0:T(8,128)} fusion(f32[4,36864]{0,1:T(8,128)} %get-tuple-element.193, s32[8192]{0:T(1024)S(1)} %bitcast_clamp_fusion.2), kind=kCustom, calls=%fused_computation.clone.1 | custom fusion | bytes 294912 | tf_op jit(solution)/shard_map/while/body/eval_jaxpr/gather | solution.py:54
  614.0 34.1 %gather_fusion = f32[8192,4]{1,0:T(8,128)} fusion(f32[4,36864]{0,1:T(8,128)} %get-tuple-element.193, s32[8192]{0:T(1024)S(1)} %bitcast_clamp_fusion.2), kind=kCustom, calls=%fused_computation.clone.1 | custom fusion | bytes 294912 | tf_op jit(solution)/shard_map/while/body/eval_jaxpr/gather | solution.py:54
  664.6 34.1 %gather_fusion = f32[8192,4]{1,0:T(8,128)} fusion(f32[4,36864]{0,1:T(8,128)} %get-tuple-element.193, s32[8192]{0:T(1024)S(1)} %bitcast_clamp_fusion.2), kind=kCustom, calls=%fused_computation.clone.1 | custom fusion | bytes 294912 | tf_op jit(solution)/shard_map/while/body/eval_jaxpr/gather | solution.py:54
  715.2 34.1 %gather_fusion = f32[8192,4]{1,0:T(8,128)} fusion(f32[4,36864]{0,1:T(8,128)} %get-tuple-element.193, s32[8192]{0:T(1024)S(1)} %bitcast_clamp_fusion.2), kind=kCustom, calls=%fused_computation.clone.1 | custom fusion | bytes 294912 | tf_op jit(solution)/shard_map/while/body/eval_jaxpr/gather | solution.py:54
  765.7 34.1 %gather_fusion = f32[8192,4]{1,0:T(8,128)} fusion(f32[4,36864]{0,1:T(8,128)} %get-tuple-element.193, s32[8192]{0:T(1024)S(1)} %bitcast_clamp_fusion.2), kind=kCustom, calls=%fused_computation.clone.1 | custom fusion | bytes 294912 | tf_op jit(solution)/shard_map/while/body/eval_jaxpr/gather | solution.py:54
  805.8 8.6 gather_fusion.1
  816.3 34.1 %gather_fusion = f32[8192,4]{1,0:T(8,128)} fusion(f32[4,36864]{0,1:T(8,128)} %get-tuple-element.193, s32[8192]{0:T(1024)S(1)} %bitcast_clamp_fusion.2), kind=kCustom, calls=%fused_computation.clone.1 | custom fusion | bytes 294912 | tf_op jit(solution)/shard_map/while/body/eval_jaxpr/gather | solution.py:54
  866.9 34.1 %gather_fusion = f32[8192,4]{1,0:T(8,128)} fusion(f32[4,36864]{0,1:T(8,128)} %get-tuple-element.193, s32[8192]{0:T(1024)S(1)} %bitcast_clamp_fusion.2), kind=kCustom, calls=%fused_computation.clone.1 | custom fusion | bytes 294912 | tf_op jit(solution)/shard_map/while/body/eval_jaxpr/gather | solution.py:54
  917.5 34.1 %gather_fusion = f32[8192,4]{1,0:T(8,128)} fusion(f32[4,36864]{0,1:T(8,128)} %get-tuple-element.193, s32[8192]{0:T(1024)S(1)} %bitcast_clamp_fusion.2), kind=kCustom, calls=%fused_computation.clone.1 | custom fusion | bytes 294912 | tf_op jit(solution)/shard_map/while/body/eval_jaxpr/gather | solution.py:54
  (463 shorter events, 277.3 us)
Async XLA Ops:
  6.5 3.7 copy-start.2
  6.5 17.6 %copy-start.5 = (s32[1,1,8]{2,1,0:T(1,128)S(1)}, s32[1,1,8]{2,1,0:T(1,128)}, u32[]{:S(2)}) copy-start(s32[1,1,8]{2,1,0:T(1,128)} %param.19) | copy-start | bytes 100
  6.5 31.1 %copy-start.3 = (f32[6,128]{1,0:T(8,128)S(1)}, f32[6,128]{1,0:T(8,128)}, u32[]{:S(2)}) copy-start(f32[6,128]{1,0:T(8,128)} %param.15) | copy-start | bytes 9220
  6.5 31.1 %copy-start.4 = (f32[3,128]{1,0:T(4,128)S(1)}, f32[3,128]{1,0:T(4,128)}, u32[]{:S(2)}) copy-start(f32[3,128]{1,0:T(4,128)} %param.14) | copy-start | bytes 4612
  6.5 31.1 %copy-start.6 = (f32[128]{0:T(128)S(1)}, f32[128]{0:T(128)}, u32[]{:S(2)}) copy-start(f32[128]{0:T(128)} %param.13) | copy-start | bytes 1540
  6.5 142.3 %all-gather.2.cloned.1.call-start = ((), (), s32[]{:S(2)}) async-start(), calls=%async_computation | async-start | bytes 2105344 | tf_op jit(solution)/shard_map/all_gather | solution.py:72
  7.6 55.3 %copy-start = (f32[3,8192]{1,0:T(4,128)S(1)}, f32[3,8192]{1,0:T(4,128)}, u32[]{:S(2)}) copy-start(f32[3,8192]{1,0:T(4,128)} %param.11) | copy-start | bytes 294916
  7.6 55.5 %copy-start.1 = (s32[128,16]{0,1:T(8,128)S(1)}, s32[128,16]{0,1:T(8,128)}, u32[]{:S(2)}) copy-start(s32[128,16]{0,1:T(8,128)} %param.17) | copy-start | bytes 24580
  24.4 13.9 %collective-permute-start = (f32[4,512]{1,0:T(4,128)S(1)}, f32[4,512]{1,0:T(4,128)S(1)}, u32[]{:S(2)}, u32[]{:S(2)}) collective-permute-start(f32[4,512]{1,0:T(4,128)S(1)} %get-tuple-element.100), channel_id=1, source_target_pairs={{16,0},{20,4},{24,8},{28,12},{32,16},{36,20},{40,24},{44,28},{48,3... | collective-permute-start | bytes 24584 | tf_op jit(solution)/shard_map/ppermute | solution.py:18
  25.7 17.0 %collective-permute-start.1 = (f32[4,512]{1,0:T(4,128)S(1)}, f32[4,512]{1,0:T(4,128)S(1)}, u32[]{:S(2)}, u32[]{:S(2)}) collective-permute-start(f32[4,512]{1,0:T(4,128)S(1)} %get-tuple-element.99), channel_id=1, source_target_pairs={{12,0},{16,4},{20,8},{24,12},{28,16},{32,20},{36,24},{40,28},{44,3... | collective-permute-start | bytes 24584 | tf_op jit(solution)/shard_map/ppermute | solution.py:18
  27.0 19.8 %collective-permute-start.2 = (f32[4,512]{1,0:T(4,128)S(1)}, f32[4,512]{1,0:T(4,128)S(1)}, u32[]{:S(2)}, u32[]{:S(2)}) collective-permute-start(f32[4,512]{1,0:T(4,128)S(1)} %get-tuple-element.98), channel_id=1, source_target_pairs={{8,0},{12,4},{16,8},{20,12},{24,16},{28,20},{32,24},{36,28},{40,32... | collective-permute-start | bytes 24584 | tf_op jit(solution)/shard_map/ppermute | solution.py:18
  28.3 34.9 %collective-permute-start.3 = (f32[4,512]{1,0:T(4,128)S(1)}, f32[4,512]{1,0:T(4,128)S(1)}, u32[]{:S(2)}, u32[]{:S(2)}) collective-permute-start(f32[4,512]{1,0:T(4,128)S(1)} %get-tuple-element.97), channel_id=1, source_target_pairs={{4,0},{8,4},{12,8},{16,12},{20,16},{24,20},{28,24},{32,28},{36,32}... | collective-permute-start | bytes 24584 | tf_op jit(solution)/shard_map/ppermute | solution.py:18
  33.5 29.8 %collective-permute-start.4 = (f32[4,512]{1,0:T(4,128)S(1)}, f32[4,512]{1,0:T(4,128)S(1)}, u32[]{:S(2)}, u32[]{:S(2)}) collective-permute-start(f32[4,512]{1,0:T(4,128)S(1)} %get-tuple-element.96), channel_id=1, source_target_pairs={{0,4},{4,8},{8,12},{12,16},{16,20},{20,24},{24,28},{28,32},{32,36}... | collective-permute-start | bytes 24584 | tf_op jit(solution)/shard_map/ppermute | solution.py:18
  38.3 25.0 %collective-permute-start.5 = (f32[4,512]{1,0:T(4,128)S(1)}, f32[4,512]{1,0:T(4,128)S(1)}, u32[]{:S(2)}, u32[]{:S(2)}) collective-permute-start(f32[4,512]{1,0:T(4,128)S(1)} %get-tuple-element.95), channel_id=1, source_target_pairs={{0,8},{4,12},{8,16},{12,20},{16,24},{20,28},{24,32},{28,36},{32,40... | collective-permute-start | bytes 24584 | tf_op jit(solution)/shard_map/ppermute | solution.py:18
  42.7 20.7 %collective-permute-start.6 = (f32[4,512]{1,0:T(4,128)S(1)}, f32[4,512]{1,0:T(4,128)S(1)}, u32[]{:S(2)}, u32[]{:S(2)}) collective-permute-start(f32[4,512]{1,0:T(4,128)S(1)} %get-tuple-element.94), channel_id=1, source_target_pairs={{0,12},{4,16},{8,20},{12,24},{16,28},{20,32},{24,36},{28,40},{32,4... | collective-permute-start | bytes 24584 | tf_op jit(solution)/shard_map/ppermute | solution.py:18
  46.8 16.5 %collective-permute-start.7 = (f32[4,512]{1,0:T(4,128)S(1)}, f32[4,512]{1,0:T(4,128)S(1)}, u32[]{:S(2)}, u32[]{:S(2)}) collective-permute-start(f32[4,512]{1,0:T(4,128)S(1)} %get-tuple-element.93), channel_id=1, source_target_pairs={{0,16},{4,20},{8,24},{12,28},{16,32},{20,36},{24,40},{28,44},{32,4... | collective-permute-start | bytes 24584 | tf_op jit(solution)/shard_map/ppermute | solution.py:18
Sparse Core Ops, SparseCore 0:
  38.4 110.3 all-gather.1
where the time goes:
time: 978 us; the launch traced here: 975 us
  local copies, waits for them, and re-layouts  774 us (79%)
  waiting for transfers between devices  75.3 us (8%)
  other arithmetic  72.5 us (7%)
  starting transfers between devices  27 us (3%)
  between operations  13.7 us (1%)
  blocking collectives  10.8 us (1%)
    gather x32, local copies, waits for them, and re-layouts, group_pull(): picked = essential[:, particle_ids]  592 us
    gather x32, local copies, waits for them, and re-layouts, group_pull(): moments = cell_table[:, cell_ids]  140 us
    all_gather x1, waiting for transfers between devices, on_device(): all_cells = lax.all_gather(cell_table, ('dom', 'sub'), axis=1, tiled=True)  75.3 us
    ppermute x8, starting transfers between devices, passed_along(): lax.ppermute(value, axis, [(source, source + steps) for source in range(l...  27 us
  transfers between devices with their start and end apart: 9, of which 1 were waited for; matrix products, arithmetic and copies ran while one was open for 1% of the time, Pallas kernels for 0%

commit v1 on v0

--- a/solution.py
+++ b/solution.py
@@ -69,7 +69,8 @@
 ):
     offset_values = list(range(-RANGE, 0)) + list(range(1, RANGE + 1))
     cell_table = jnp.concatenate([cell_mass[None], cell_center, cell_quad], axis=0)
-    all_cells = lax.all_gather(cell_table, ("dom", "sub"), axis=1, tiled=True)
+    repeated = jnp.stack([cell_table] * lax.axis_size(("dom", "sub")))
+    all_cells = jnp.concatenate(lax.all_to_all(repeated, ("dom", "sub"), 0, 0), axis=1)
     packed = jnp.concatenate([positions, masses[None]], axis=0)
     nearby = lax.all_gather(packed, "sub", axis=1, tiled=True)
     chosen = send_list.reshape(2 * RANGE, CAP)

time: 978 us -> 930 us (0.951)
  waiting for transfers between devices: 75.3 us -> 17.8 us
  starting transfers between devices: 27 us -> 44 us
  between operations: 13.7 us -> 0.3 us
    all_gather x1 -> x0, waiting for transfers between devices: 75.3 us -> none  [on_device(): all_cells = lax.all_gather(cell_table, ('dom', 'sub'), axis=1, tiled=True)]
    all_to_all x0 -> x1, starting transfers between devices: none -> 17.5 us  [on_device(): lax.all_to_all(repeated, ('dom', 'sub'), 0, 0)]
  transfers between devices with their start and end apart: 9 -> 9, of which waited for: 1 -> 4; matrix products, arithmetic and copies ran while one was open for 1% -> 1% of each run, Pallas kernels for 0% -> 0%
where the time goes in v1:
time: 930 us; the launch traced here: 924 us
  local copies, waits for them, and re-layouts  774 us (83%)
  other arithmetic  71.9 us (8%)
  starting transfers between devices  44 us (5%)
  waiting for transfers between devices  17.8 us (2%)
  blocking collectives  13.4 us (1%)
    gather x32, local copies, waits for them, and re-layouts, group_pull(): picked = essential[:, particle_ids]  592 us
    gather x32, local copies, waits for them, and re-layouts, group_pull(): moments = cell_table[:, cell_ids]  140 us
    ppermute x8, starting transfers between devices, passed_along(): lax.ppermute(value, axis, [(source, source + steps) for source in range(l...  26.5 us
    while x2, local copies, waits for them, and re-layouts, on_device(): pulled = lax.map(one_block, (target_blocks, leaf_blocks, cell_blocks))  18.8 us
  transfers between devices with their start and end apart: 9, of which 4 were waited for; matrix products, arithmetic and copies ran while one was open for 1% of the time, Pallas kernels for 0%

profile of v1, /device:TPU:1, one launch (start us, length us, event | category | flops | bytes accessed | tf_op | source)
XLA Modules:
  0.0 924.1 jit_solution(10534818323463038066)
XLA Ops:
  4.0 12.9 %gather_fusion.2 = f32[4096,4]{1,0:T(8,128)S(1)} fusion(f32[4,8192]{0,1:T(8,128)} %copy.59, s32[4096]{0:T(1024)S(1)} %broadcast_clamp_fusion), kind=kCustom, calls=%fused_computation.2 | custom fusion | bytes 147456 | tf_op jit(solution)/shard_map/gather | solution.py:83
  32.6 17.5 %all-to-all-start = ((f32[256,10,128]{2,1,0:T(8,128)}), f32[256,10,128]{2,1,0:T(8,128)S(1)}, u32[]{:S(2)}, u32[]{:S(2)}) async-start(f32[256,10,128]{2,1,0:T(8,128)} %stack.31), calls=%async_computation | async-start | bytes 4194304 | tf_op jit(solution)/shard_map/all_to_all | solution.py:73
  63.4 13.4 %all_gather.3 = f32[4,32768]{1,0:T(4,128)S(1)} all-gather(f32[4,8192]{1,0:T(4,128)S(1)} %pad_maximum_fusion.2), channel_id=1, replica_groups=mesh['dom'=64,'sub'=4] {'sub'}, dimensions={1}, use_global_device_ids=true | all-gather | bytes 655360 | tf_op jit(solution)/shard_map/all_gather | solution.py:75
  77.1 9.0 collective-permute-done.5
  86.9 9.8 %copy.69 = f32[4,36864]{0,1:T(8,128)} copy(f32[4,36864]{1,0:T(4,128)S(1)} %pad_maximum_fusion.1) | data formatting | bytes 1179648 | tf_op jit(solution)/shard_map/while | solution.py:99
  105.0 9.0 copy.73
  114.0 809.3 %while.10 = (s32[]{:T(128)}, f32[16,3,8,64]{3,2,1,0:T(8,128)S(1)}, s32[16,8,16]{2,1,0:T(8,128)S(1)}, f32[4,36864]{0,1:T(8,128)}, f32[16,3,8,64]{3,2,0,1:T(8,128)...) while((s32[]{:T(128)}, f32[16,3,8,64]{3,2,1,0:T(8,128)S(1)}, s32[16,8,16]{2,1,0:T(8,128)S(1)}, ...), condition=%wide.region_6.7_spmd, body=%wide.region_0.6_spmd.sunk | while | flops 15249026 | bytes 16653933 | solution.py:99
  114.3 34.1 %gather_fusion = f32[8192,4]{1,0:T(8,128)} fusion(f32[4,36864]{0,1:T(8,128)} %get-tuple-element.200, s32[8192]{0:T(1024)S(1)} %bitcast_clamp_fusion.2), kind=kCustom, calls=%fused_computation.clone.1 | custom fusion | bytes 294912 | tf_op jit(solution)/shard_map/while/body/eval_jaxpr/gather | solution.py:54
  164.9 34.1 %gather_fusion = f32[8192,4]{1,0:T(8,128)} fusion(f32[4,36864]{0,1:T(8,128)} %get-tuple-element.200, s32[8192]{0:T(1024)S(1)} %bitcast_clamp_fusion.2), kind=kCustom, calls=%fused_computation.clone.1 | custom fusion | bytes 294912 | tf_op jit(solution)/shard_map/while/body/eval_jaxpr/gather | solution.py:54
  215.5 34.1 %gather_fusion = f32[8192,4]{1,0:T(8,128)} fusion(f32[4,36864]{0,1:T(8,128)} %get-tuple-element.200, s32[8192]{0:T(1024)S(1)} %bitcast_clamp_fusion.2), kind=kCustom, calls=%fused_computation.clone.1 | custom fusion | bytes 294912 | tf_op jit(solution)/shard_map/while/body/eval_jaxpr/gather | solution.py:54
  266.0 34.1 %gather_fusion = f32[8192,4]{1,0:T(8,128)} fusion(f32[4,36864]{0,1:T(8,128)} %get-tuple-element.200, s32[8192]{0:T(1024)S(1)} %bitcast_clamp_fusion.2), kind=kCustom, calls=%fused_computation.clone.1 | custom fusion | bytes 294912 | tf_op jit(solution)/shard_map/while/body/eval_jaxpr/gather | solution.py:54
  316.6 34.1 %gather_fusion = f32[8192,4]{1,0:T(8,128)} fusion(f32[4,36864]{0,1:T(8,128)} %get-tuple-element.200, s32[8192]{0:T(1024)S(1)} %bitcast_clamp_fusion.2), kind=kCustom, calls=%fused_computation.clone.1 | custom fusion | bytes 294912 | tf_op jit(solution)/shard_map/while/body/eval_jaxpr/gather | solution.py:54
  367.2 34.1 %gather_fusion = f32[8192,4]{1,0:T(8,128)} fusion(f32[4,36864]{0,1:T(8,128)} %get-tuple-element.200, s32[8192]{0:T(1024)S(1)} %bitcast_clamp_fusion.2), kind=kCustom, calls=%fused_computation.clone.1 | custom fusion | bytes 294912 | tf_op jit(solution)/shard_map/while/body/eval_jaxpr/gather | solution.py:54
  407.3 8.6 gather_fusion.1
  417.8 34.1 %gather_fusion = f32[8192,4]{1,0:T(8,128)} fusion(f32[4,36864]{0,1:T(8,128)} %get-tuple-element.200, s32[8192]{0:T(1024)S(1)} %bitcast_clamp_fusion.2), kind=kCustom, calls=%fused_computation.clone.1 | custom fusion | bytes 294912 | tf_op jit(solution)/shard_map/while/body/eval_jaxpr/gather | solution.py:54
  468.4 34.1 %gather_fusion = f32[8192,4]{1,0:T(8,128)} fusion(f32[4,36864]{0,1:T(8,128)} %get-tuple-element.200, s32[8192]{0:T(1024)S(1)} %bitcast_clamp_fusion.2), kind=kCustom, calls=%fused_computation.clone.1 | custom fusion | bytes 294912 | tf_op jit(solution)/shard_map/while/body/eval_jaxpr/gather | solution.py:54
  518.9 34.1 %gather_fusion = f32[8192,4]{1,0:T(8,128)} fusion(f32[4,36864]{0,1:T(8,128)} %get-tuple-element.200, s32[8192]{0:T(1024)S(1)} %bitcast_clamp_fusion.2), kind=kCustom, calls=%fused_computation.clone.1 | custom fusion | bytes 294912 | tf_op jit(solution)/shard_map/while/body/eval_jaxpr/gather | solution.py:54
  569.5 34.1 %gather_fusion = f32[8192,4]{1,0:T(8,128)} fusion(f32[4,36864]{0,1:T(8,128)} %get-tuple-element.200, s32[8192]{0:T(1024)S(1)} %bitcast_clamp_fusion.2), kind=kCustom, calls=%fused_computation.clone.1 | custom fusion | bytes 294912 | tf_op jit(solution)/shard_map/while/body/eval_jaxpr/gather | solution.py:54
  620.1 34.1 %gather_fusion = f32[8192,4]{1,0:T(8,128)} fusion(f32[4,36864]{0,1:T(8,128)} %get-tuple-element.200, s32[8192]{0:T(1024)S(1)} %bitcast_clamp_fusion.2), kind=kCustom, calls=%fused_computation.clone.1 | custom fusion | bytes 294912 | tf_op jit(solution)/shard_map/while/body/eval_jaxpr/gather | solution.py:54
  670.7 34.1 %gather_fusion = f32[8192,4]{1,0:T(8,128)} fusion(f32[4,36864]{0,1:T(8,128)} %get-tuple-element.200, s32[8192]{0:T(1024)S(1)} %bitcast_clamp_fusion.2), kind=kCustom, calls=%fused_computation.clone.1 | custom fusion | bytes 294912 | tf_op jit(solution)/shard_map/while/body/eval_jaxpr/gather | solution.py:54
  721.3 34.1 %gather_fusion = f32[8192,4]{1,0:T(8,128)} fusion(f32[4,36864]{0,1:T(8,128)} %get-tuple-element.200, s32[8192]{0:T(1024)S(1)} %bitcast_clamp_fusion.2), kind=kCustom, calls=%fused_computation.clone.1 | custom fusion | bytes 294912 | tf_op jit(solution)/shard_map/while/body/eval_jaxpr/gather | solution.py:54
  771.9 34.1 %gather_fusion = f32[8192,4]{1,0:T(8,128)} fusion(f32[4,36864]{0,1:T(8,128)} %get-tuple-element.200, s32[8192]{0:T(1024)S(1)} %bitcast_clamp_fusion.2), kind=kCustom, calls=%fused_computation.clone.1 | custom fusion | bytes 294912 | tf_op jit(solution)/shard_map/while/body/eval_jaxpr/gather | solution.py:54
  822.4 34.1 %gather_fusion = f32[8192,4]{1,0:T(8,128)} fusion(f32[4,36864]{0,1:T(8,128)} %get-tuple-element.200, s32[8192]{0:T(1024)S(1)} %bitcast_clamp_fusion.2), kind=kCustom, calls=%fused_computation.clone.1 | custom fusion | bytes 294912 | tf_op jit(solution)/shard_map/while/body/eval_jaxpr/gather | solution.py:54
  873.0 34.1 %gather_fusion = f32[8192,4]{1,0:T(8,128)} fusion(f32[4,36864]{0,1:T(8,128)} %get-tuple-element.200, s32[8192]{0:T(1024)S(1)} %bitcast_clamp_fusion.2), kind=kCustom, calls=%fused_computation.clone.1 | custom fusion | bytes 294912 | tf_op jit(solution)/shard_map/while/body/eval_jaxpr/gather | solution.py:54
  (465 shorter events, 295.0 us)
Async XLA Ops:
  0.0 3.7 copy-start.3
  0.0 17.6 %copy-start.6 = (s32[1,1,8]{2,1,0:T(1,128)S(1)}, s32[1,1,8]{2,1,0:T(1,128)}, u32[]{:S(2)}) copy-start(s32[1,1,8]{2,1,0:T(1,128)} %param.19) | copy-start | bytes 100
  0.0 31.1 %copy-start.4 = (f32[6,128]{1,0:T(8,128)S(1)}, f32[6,128]{1,0:T(8,128)}, u32[]{:S(2)}) copy-start(f32[6,128]{1,0:T(8,128)} %param.15) | copy-start | bytes 9220
  0.0 31.1 %copy-start.5 = (f32[3,128]{1,0:T(4,128)S(1)}, f32[3,128]{1,0:T(4,128)}, u32[]{:S(2)}) copy-start(f32[3,128]{1,0:T(4,128)} %param.14) | copy-start | bytes 4612
  0.0 31.1 %copy-start.7 = (f32[128]{0:T(128)S(1)}, f32[128]{0:T(128)}, u32[]{:S(2)}) copy-start(f32[128]{0:T(128)} %param.13) | copy-start | bytes 1540
  17.6 59.2 %copy-start = (f32[3,8192]{1,0:T(4,128)S(1)}, f32[3,8192]{1,0:T(4,128)}, u32[]{:S(2)}) copy-start(f32[3,8192]{1,0:T(4,128)} %param.11) | copy-start | bytes 294916
  17.6 59.4 %copy-start.2 = (s32[128,16]{0,1:T(8,128)S(1)}, s32[128,16]{0,1:T(8,128)}, u32[]{:S(2)}) copy-start(s32[128,16]{0,1:T(8,128)} %param.17) | copy-start | bytes 24580
  17.8 32.2 %collective-permute-start = (f32[4,512]{1,0:T(4,128)S(1)}, f32[4,512]{1,0:T(4,128)S(1)}, u32[]{:S(2)}, u32[]{:S(2)}) collective-permute-start(f32[4,512]{1,0:T(4,128)S(1)} %get-tuple-element.107), channel_id=1, source_target_pairs={{16,0},{20,4},{24,8},{28,12},{32,16},{36,20},{40,24},{44,28},{48,3... | collective-permute-start | bytes 24584 | tf_op jit(solution)/shard_map/ppermute | solution.py:18
  19.1 34.3 %collective-permute-start.1 = (f32[4,512]{1,0:T(4,128)S(1)}, f32[4,512]{1,0:T(4,128)S(1)}, u32[]{:S(2)}, u32[]{:S(2)}) collective-permute-start(f32[4,512]{1,0:T(4,128)S(1)} %get-tuple-element.106), channel_id=1, source_target_pairs={{12,0},{16,4},{20,8},{24,12},{28,16},{32,20},{36,24},{40,28},{44,3... | collective-permute-start | bytes 24584 | tf_op jit(solution)/shard_map/ppermute | solution.py:18
  20.4 38.1 %collective-permute-start.2 = (f32[4,512]{1,0:T(4,128)S(1)}, f32[4,512]{1,0:T(4,128)S(1)}, u32[]{:S(2)}, u32[]{:S(2)}) collective-permute-start(f32[4,512]{1,0:T(4,128)S(1)} %get-tuple-element.105), channel_id=1, source_target_pairs={{8,0},{12,4},{16,8},{20,12},{24,16},{28,20},{32,24},{36,28},{40,32... | collective-permute-start | bytes 24584 | tf_op jit(solution)/shard_map/ppermute | solution.py:18
  21.7 55.3 %collective-permute-start.3 = (f32[4,512]{1,0:T(4,128)S(1)}, f32[4,512]{1,0:T(4,128)S(1)}, u32[]{:S(2)}, u32[]{:S(2)}) collective-permute-start(f32[4,512]{1,0:T(4,128)S(1)} %get-tuple-element.104), channel_id=1, source_target_pairs={{4,0},{8,4},{12,8},{16,12},{20,16},{24,20},{28,24},{32,28},{36,32}... | collective-permute-start | bytes 24584 | tf_op jit(solution)/shard_map/ppermute | solution.py:18
  26.9 50.2 %collective-permute-start.4 = (f32[4,512]{1,0:T(4,128)S(1)}, f32[4,512]{1,0:T(4,128)S(1)}, u32[]{:S(2)}, u32[]{:S(2)}) collective-permute-start(f32[4,512]{1,0:T(4,128)S(1)} %get-tuple-element.103), channel_id=1, source_target_pairs={{0,4},{4,8},{8,12},{12,16},{16,20},{20,24},{24,28},{28,32},{32,36}... | collective-permute-start | bytes 24584 | tf_op jit(solution)/shard_map/ppermute | solution.py:18
  32.6 72.5 %all-to-all-start = ((f32[256,10,128]{2,1,0:T(8,128)}), f32[256,10,128]{2,1,0:T(8,128)S(1)}, u32[]{:S(2)}, u32[]{:S(2)}) async-start(f32[256,10,128]{2,1,0:T(8,128)} %stack.31), calls=%async_computation | async-start | bytes 4194304 | tf_op jit(solution)/shard_map/all_to_all | solution.py:73
  50.0 36.1 %collective-permute-start.5 = (f32[4,512]{1,0:T(4,128)S(1)}, f32[4,512]{1,0:T(4,128)S(1)}, u32[]{:S(2)}, u32[]{:S(2)}) collective-permute-start(f32[4,512]{1,0:T(4,128)S(1)} %get-tuple-element.102), channel_id=1, source_target_pairs={{0,8},{4,12},{8,16},{12,20},{16,24},{20,28},{24,32},{28,36},{32,40... | collective-permute-start | bytes 24584 | tf_op jit(solution)/shard_map/ppermute | solution.py:18
  53.5 32.9 %collective-permute-start.6 = (f32[4,512]{1,0:T(4,128)S(1)}, f32[4,512]{1,0:T(4,128)S(1)}, u32[]{:S(2)}, u32[]{:S(2)}) collective-permute-start(f32[4,512]{1,0:T(4,128)S(1)} %get-tuple-element.101), channel_id=1, source_target_pairs={{0,12},{4,16},{8,20},{12,24},{16,28},{20,32},{24,36},{28,40},{32,4... | collective-permute-start | bytes 24584 | tf_op jit(solution)/shard_map/ppermute | solution.py:18
  58.5 28.1 %collective-permute-start.7 = (f32[4,512]{1,0:T(4,128)S(1)}, f32[4,512]{1,0:T(4,128)S(1)}, u32[]{:S(2)}, u32[]{:S(2)}) collective-permute-start(f32[4,512]{1,0:T(4,128)S(1)} %get-tuple-element.100), channel_id=1, source_target_pairs={{0,16},{4,20},{8,24},{12,28},{16,32},{20,36},{24,40},{28,44},{32,4... | collective-permute-start | bytes 24584 | tf_op jit(solution)/shard_map/ppermute | solution.py:18
  105.0 9.0 copy-start.1
